TPU v7x, 32 devices: a whole 2x2x4 slice. The times are simulated.
32 devices in a mesh: slab: 8 (over z, x), hodlr: 4 (over y, core).
Axes of the slice: x: 2, y: 2, z: 4, core: 2. Of those that a mesh axis runs over, the one named last changes fastest.
Arguments:
- sources: bfloat16 [8, 32, 16384], P('slab', None, 'hodlr'), may hold values from -2 to 2
- leaves: bfloat16 [8, 16, 1024, 1024], P('slab', 'hodlr'), may hold values from -1 to 2
- v_rows: bfloat16 [8, 4, 64, 16384], P('slab', None, None, 'hodlr'), may hold values from -0.0625 to 0.0625
- u_rows: bfloat16 [8, 4, 64, 16384], P('slab', None, None, 'hodlr'), may hold values from -0.1875 to 0.1875
Outputs:
- fronts: bfloat16 [8, 32, 16384], P('slab', None, 'hodlr')
All inputs are finite; a program needn't handle non-finite values.
Results may differ from a plain program's by a relative error of at most 0.025.
Values may be sent and summed in bfloat16 or wider, within the bound.
No kernel may reach another device: no remote copies, remote signals or barrier semaphores. Data moves between devices by JAX's collectives and lax.ppermute only.
A program may use at most 64 MiB of HBM per device.

v0:
```python
import functools

import jax
import jax.numpy as jnp
from jax import lax
from jax.experimental import pallas as pl
from jax.experimental.pallas import tpu as pltpu
from jax.sharding import PartitionSpec as P

VMEM_LIMIT = 24 * 1024 * 1024
FIRST_SHARE = 2
SPLIT_HOPS = 3
IN_PLACE = 2
OPEN_FLOPS = 4 * 10**9
ROWS_TIMES_COLUMNS = (((1,), (0,)), ((), ()))
ROWS_TIMES_ROWS = (((1,), (1,)), ((), ()))


def dot(a, b, dims=ROWS_TIMES_COLUMNS):
    return lax.dot_general(a, b, dims, preferred_element_type=jnp.float32)


def call(kernel, outs, args, aliases=None, scratch=(), from_hbm=(), flops=0):
    whole = pl.BlockSpec(memory_space=pltpu.VMEM)
    remote = pl.BlockSpec(memory_space=pl.ANY)
    placed = [
        pltpu.with_memory_space_constraint(a, pltpu.HBM if i in from_hbm else pltpu.VMEM)
        for i, a in enumerate(args)
    ]
    return pl.pallas_call(
        kernel,
        out_shape=outs,
        in_specs=[remote if i in from_hbm else whole for i in range(len(args))],
        out_specs=[whole] * len(outs),
        scratch_shapes=scratch,
        input_output_aliases=aliases or {},
        compiler_params=pltpu.CompilerParams(vmem_limit_bytes=VMEM_LIMIT),
        cost_estimate=pl.CostEstimate(flops=flops, bytes_accessed=0, transcendentals=0),
    )(*placed)


def on_factors(value, v_refs, columns, ranks):
    pieces = [dot(value, ref[:, columns], ROWS_TIMES_ROWS) for ref in v_refs]
    missing = ranks - sum(ref.shape[0] for ref in v_refs)
    if missing:
        pieces.append(jnp.zeros((value.shape[0], missing), jnp.float32))
    return jnp.concatenate(pieces, axis=1)


def fetch_kernel(spans, factors, source_ref, v_ref, *refs):
    v_outs, w_outs, sems = refs[:factors], refs[factors:-1], refs[-1]
    copies, level = [], 0
    for out in v_outs:
        copies.append((v_ref.at[pl.ds(level, out.shape[0])], out))
        level += out.shape[0]
    for out, (start, stop) in zip(w_outs, spans):
        copies.append((source_ref.at[:, pl.ds(start, stop - start)], out))
    copies = [pltpu.make_async_copy(a, b, sems.at[i]) for i, (a, b) in enumerate(copies)]
    for copy in copies:
        copy.start()
    for copy in copies:
        copy.wait()


def fetch(spans, shares, source, v):
    _, rank, width = v.shape
    outs = [pltpu.VMEM((n, rank, width), v.dtype) for n in shares]
    outs += [pltpu.VMEM((source.shape[0], stop - start), source.dtype) for start, stop in spans]
    found = call(
        functools.partial(fetch_kernel, spans, len(shares)),
        outs,
        [source, v],
        scratch=[pltpu.SemaphoreType.DMA((len(outs),))],
        from_hbm=(0, 1),
    )
    return [f.reshape(-1, width) for f in found[: len(shares)]], list(found[len(shares) :])


def project_kernel(spans, factors, *refs):
    v_refs, parts, p_ref = refs[:factors], refs[factors:-1], refs[-1]
    total = None
    for ref, (start, stop) in zip(parts, spans):
        term = on_factors(ref[...], v_refs, slice(start, stop), p_ref.shape[1])
        total = term if total is None else total + term
    p_ref[...] = total


def project(spans, w, far_v, ranks, flops=0):
    outs = [pltpu.VMEM((w[0].shape[0], ranks), jnp.float32)]
    return call(functools.partial(project_kernel, spans, len(far_v)), outs, [*far_v, *w], flops=flops)[0]


def leaves_of(span, size):
    return range(span[0] // size, span[1] // size)


def first_kernel(spans, cross, *refs):
    n = len(spans)
    w_refs, (leaf_ref, v_ref), near_out = refs[:n], refs[n : n + 2], refs[n + 2]
    sum_refs, p_refs = refs[n + 3 : 2 * n + 3], refs[2 * n + 3 :]
    size = leaf_ref.shape[1]
    near = near_out.shape[1]
    for i, span in enumerate(spans):
        for j, c in enumerate(leaves_of(span, size)):
            columns = slice(j * size, (j + 1) * size)
            turned = v_ref[cross:, :, c * size : (c + 1) * size].reshape(near, size).T
            near_out[c * size : (c + 1) * size, :] = turned
            p_refs[i][j] = dot(w_refs[i][:, columns], turned)
            sum_refs[i][:, columns] = dot(w_refs[i][:, columns], leaf_ref[c])


def first_part(spans, cross, w, leaf, v):
    levels, rank, width = v.shape
    size = leaf.shape[1]
    rows = w[0].shape[0]
    near = (levels - cross) * rank
    outs = [pltpu.VMEM((width, near), v.dtype)]
    outs += [pltpu.VMEM(x.shape, jnp.float32) for x in w]
    outs += [pltpu.VMEM((x.shape[1] // size, rows, near), jnp.float32) for x in w]
    n = len(w)
    found = call(functools.partial(first_kernel, spans, cross), outs, [*w, leaf, v])
    return found[0], list(found[1 : 1 + n]), list(found[1 + n :])


def nearby_kernel(front_ref, v_ref, *refs):
    p_ref = refs[-1]
    term = dot(front_ref[...], v_ref[...], ROWS_TIMES_ROWS)
    before = p_ref.shape[1] - term.shape[1]
    if before:
        term = jnp.concatenate([jnp.zeros((term.shape[0], before), jnp.float32), term], axis=1)
    p_ref[...] = term


def nearby_part(front, v, ranks, behind):
    outs = [pltpu.VMEM((front.shape[0], ranks), jnp.float32)]
    return call(nearby_kernel, outs, [front, v, *behind])[0]


def near_kernel(span, start, w_ref, front_ref, leaf_ref, v_ref, *refs):
    w_out, sum_out, p_out = refs[-3:]
    size = leaf_ref.shape[1]
    for j, c in enumerate(leaves_of(span, size)):
        columns = slice(j * size, (j + 1) * size)
        w = w_ref[:, columns] + front_ref[:, start + j * size : start + (j + 1) * size]
        w_out[:, columns] = w
        p_out[j] = dot(w, v_ref[c * size : (c + 1) * size, :])
        sum_out[:, columns] = dot(w, leaf_ref[c])


def near_part(span, start, w, front, leaf, near_v, behind):
    outs = [
        pltpu.VMEM(w.shape, w.dtype),
        pltpu.VMEM(w.shape, jnp.float32),
        pltpu.VMEM((w.shape[1] // leaf.shape[1], w.shape[0], near_v.shape[1]), jnp.float32),
    ]
    return call(functools.partial(near_kernel, span, start), outs, [w, front, leaf, near_v, *behind], {0: 0})


def far_kernel(rank, size, spans, chosen, levels_of, *refs):
    refs = list(refs)
    sum_refs = [refs.pop(0) for _ in chosen]
    p_refs = [refs.pop(0) for _ in spans]
    q_ref = refs.pop(0)
    part_refs = [refs.pop(0) for _ in levels_of]
    u_ref = refs.pop(0)
    out_ref, q_out = refs[:2]
    rows, far = q_ref.shape
    near = u_ref.shape[0] - far

    q = q_ref[...]
    lane = lax.broadcasted_iota(jnp.int32, (rows, far), 1) // rank
    for ref, level in zip(part_refs, levels_of):
        q = q + jnp.where(lane == level, ref[...], 0.0)
    q_out[...] = q

    projected = [ref[j] for ref in p_refs for j in range(ref.shape[0])]
    nleaf = len(projected)
    lane = lax.broadcasted_iota(jnp.int32, (rows, near), 1) // rank
    sums = []
    for level in range(near // rank):
        block = nleaf >> (level + 1)
        sums.append(
            [
                functools.reduce(jnp.add, projected[b * block : (b + 1) * block])
                for b in range(nleaf // block)
            ]
        )
    place = 0
    for i, ref in zip(chosen, sum_refs):
        for j, c in enumerate(leaves_of(spans[i], size)):
            swapped = sums[0][(c // (nleaf >> 1)) ^ 1]
            for level in range(1, near // rank):
                swapped = jnp.where(lane == level, sums[level][(c // (nleaf >> (level + 1))) ^ 1], swapped)
            columns = slice(c * size, (c + 1) * size)
            value = ref[:, j * size : (j + 1) * size]
            value = value + dot(q.astype(jnp.bfloat16), u_ref[:far, columns])
            value = value + dot(swapped.astype(jnp.bfloat16), u_ref[far:, columns])
            out_ref[:, place : place + size] = value.astype(jnp.bfloat16)
            place += size


def far_part(rank, size, spans, chosen, sums, projected, q, parts, levels_of, u, last):
    args = [*[sums[i] for i in chosen], *projected, q, *parts, u]
    width = sum(sums[i].shape[1] for i in chosen)
    space = jax.ShapeDtypeStruct if last else pltpu.VMEM
    outs = [space((q.shape[0], width), jnp.bfloat16), pltpu.VMEM(q.shape, jnp.float32)]
    kernel = functools.partial(far_kernel, rank, size, spans, chosen, tuple(levels_of) if parts else ())
    return call(kernel, outs, args, {len(chosen) + len(projected): 1})


def local(sources, leaves, v_rows, u_rows):
    devices = lax.axis_size("hodlr")
    chain = lax.axis_size("slab")
    cross = devices.bit_length() - 1
    source, right = sources[0], v_rows[0]
    levels, rank, width = right.shape
    nleaf, size = leaves.shape[1:3]
    cut = max(nleaf * FIRST_SHARE // 4, 1) * size
    spans = ((0, cut), (cut, width))
    offsets = list(range(1, devices))
    levels_of = [cross - x.bit_length() for x in offsets]

    def moved(x, moves, offset=0):
        route = [(a * devices + h, b * devices + (h ^ offset)) for a, b in moves for h in range(devices)]
        return lax.ppermute(x, ("slab", "hodlr"), route)

    def exchanged(p, moves):
        return [moved(p, moves, x) for x in offsets]

    shares = [n for n in (cross - 1, 1) if n]
    far_v, w = fetch(spans, shares, source, right)
    shifted = [
        moved(v, [(k, k - 1) for k in range(IN_PLACE + 1 if v is far_v[-1] else 1, chain)]) for v in far_v
    ]
    ranks = cross * rank
    whole = ((0, width),)
    p = project(spans, w, far_v, ranks, OPEN_FLOPS)
    parts = exchanged(p, [(k, k) for k in range(chain)])
    leaf, u = leaves[0], u_rows[0].reshape(levels * rank, width)
    near_v, sums, projected = first_part(spans, cross, w, leaf, right)

    q = jnp.zeros(p.shape, jnp.float32)
    every = tuple(range(len(spans)))
    far = functools.partial(far_part, rank, size, spans)
    out, q = far(every, sums, projected, q, parts, levels_of, u, False)
    front = [moved(out, [(0, 1)])]
    ahead = [project(whole, [out], shifted[:-1], ranks)] if cross > 1 else []
    parts = [moved(ahead[0], [(0, 1)], x) for x in offsets[1:]]
    for k in range(1, chain):
        first = []
        if k <= IN_PLACE:
            first = parts
            nearby = nearby_part(front[0], far_v[-1], ranks, ahead if k == 1 else shifted[-1:])
            parts = [moved(nearby, [(k, k)], offsets[0])] + parts
        for i, span in enumerate(spans):
            behind = projected[i - 1 : i] if i else first
            given, start = (front[0], span[0]) if len(front) == 1 else (front[i], 0)
            w[i], sums[i], projected[i] = near_part(span, start, w[i], given, leaf, near_v, behind)
        if k == chain - 1:
            out, _ = far(every, sums, projected, q, parts, levels_of, u, True)
            return out[None]
        split = k >= chain - 1 - SPLIT_HOPS
        outs, front = [], []
        for chosen in [(i,) for i in every] if split else [every]:
            out, q = far(chosen, sums, projected, q, [] if front else parts, levels_of, u, False)
            outs.append(out)
            front.append(moved(out, [(k, k + 1)]))
        following = shifted[:-1] if k < IN_PLACE else shifted
        p = project(spans if split else whole, outs, following, ranks)
        parts = [moved(p, [(k, k + 1)], x) for x in offsets[1 if k < IN_PLACE else 0 :]]


def solution(mesh):
    in_specs = (
        P("slab", None, "hodlr"),
        P("slab", "hodlr", None, None),
        P("slab", None, None, "hodlr"),
        P("slab", None, None, "hodlr"),
    )
    out_specs = P("slab", None, "hodlr")
    return jax.shard_map(local, mesh=mesh, in_specs=in_specs, out_specs=out_specs, check_vma=False)
```

profile of v0, /device:TPU:26, one launch (start us, length us, event | category | flops | bytes accessed | tf_op | source)
XLA Modules:
  0.0 97.2 jit_solution(18339479633291194795)
XLA Ops:
  0.0 1.4 %shard_map.46 = (bf16[1,64,4096]{2,1,0:T(8,128)(2,1)S(1)}, bf16[1,64,4096]{2,1,0:T(8,128)(2,1)S(1)}, bf16[32,2048]{1,0:T(8,128)(2,1)S(1)}, bf16[32,2048]{1,0:T(8,128)(2,1)S(1)}) custom-call(bf16[32,4096]{1,0:T(8,128)(2,1)} %bitcast.43, bf16[4,64,4096]{2,1,0:T(8,128)(2,1)} %bitcast.35), custom_call_target="tpu_custom_call" | custom-call | tf_op jit(solution)/shard_map/pallas_call | solution.py:30
  1.5 2.6 %collective-permute-start.4 = (bf16[64,4096]{1,0:T(8,128)(2,1)S(1)}, bf16[64,4096]{1,0:T(8,128)(2,1)S(1)}, u32[]{:S(2)}, u32[]{:S(2)}) collective-permute-start(bf16[64,4096]{1,0:T(8,128)(2,1)S(1)} %bitcast.41), channel_id=1, source_target_pairs={{4,0},{5,1},{6,2},{7,3},{8,4},{9,5},{10,6},{11,7},{12,8},{13,9},{1... | collective-permute-start | bytes 1572872 | tf_op jit(solution)/shard_map/ppermute | solution.py:225
  4.1 0.4 shard_map.48
  4.6 1.6 %collective-permute-start.1 = (f32[32,128]{1,0:T(8,128)S(1)}, f32[32,128]{1,0:T(8,128)S(1)}, u32[]{:S(2)}, u32[]{:S(2)}) collective-permute-start(f32[32,128]{1,0:T(8,128)S(1)} %shard_map.48), channel_id=1, source_target_pairs={{0,2},{1,3},{2,0},{3,1},{4,6},{5,7},{6,4},{7,5},{8,10},{9,11},{10,... | collective-permute-start | bytes 49160 | tf_op jit(solution)/shard_map/ppermute | solution.py:225
  6.5 0.5 copy-done.1
  6.9 1.8 %shard_map.47 = (bf16[4096,128]{1,0:T(8,128)(2,1)S(1)}, f32[32,2048]{1,0:T(8,128)S(1)}, f32[32,2048]{1,0:T(8,128)S(1)}, f32[2,32,128]{2,1,0:T(8,128)S(1)}, f32[2,32,128]{2,1,0:T(8,128)S(1)}) custom-call(bf16[32,2048]{1,0:T(8,128)(2,1)S(1)} %get-tuple-element.75.refs_0_.refs_2_.w_ref, bf16[32,2048]{1,0:T(8,128)(2,1)S(1)} %get-tuple-element.76.refs_1_.refs_3_.w_ref, ...), custom_call_target="tpu_custom_call" | custom-call | tf_op jit(solution)/shard_map/pallas_call | solution.py:30
  8.8 0.6 collective-permute-done.2.refs_7_
  9.7 0.7 collective-permute-start.3
  10.4 3.3 %collective-permute-start.11 = (bf16[64,4096]{1,0:T(8,128)(2,1)S(1)}, bf16[64,4096]{1,0:T(8,128)(2,1)S(1)}, u32[]{:S(2)}, u32[]{:S(2)}) collective-permute-start(bf16[64,4096]{1,0:T(8,128)(2,1)S(1)} %bitcast.38), channel_id=1, source_target_pairs={{12,8},{13,9},{14,10},{15,11},{16,12},{17,13},{18,14},{19,15},{20,... | collective-permute-start | bytes 1572872 | tf_op jit(solution)/shard_map/ppermute | solution.py:225
  13.7 2.3 %collective-permute-done.4.refs_0_ = bf16[64,4096]{1,0:T(8,128)(2,1)S(1)} collective-permute-done((bf16[64,4096]{1,0:T(8,128)(2,1)S(1)}, bf16[64,4096]{1,0:T(8,128)(2,1)S(1)}, u32[]{:S(2)}, u32[]{:S(2)}) %collective-permute-start.4) | collective-permute-done | bytes 524320 | tf_op jit(solution)/shard_map/ppermute | solution.py:225
  16.3 0.7 collective-permute-start.5
  17.0 0.7 collective-permute-start.6
  18.0 0.7 collective-permute-start.7
  18.7 0.9 shard_map.51
  19.6 0.9 shard_map.52
  20.5 0.4 shard_map.54
  21.0 0.7 collective-permute-start.8
  21.9 0.7 collective-permute-start.10
  22.6 0.7 collective-permute-start.9
  23.3 3.2 %collective-permute-done.11.refs_0_.refs_1_ = bf16[64,4096]{1,0:T(8,128)(2,1)S(1)} collective-permute-done((bf16[64,4096]{1,0:T(8,128)(2,1)S(1)}, bf16[64,4096]{1,0:T(8,128)(2,1)S(1)}, u32[]{:S(2)}, u32[]{:S(2)}) %collective-permute-start.11) | collective-permute-done | bytes 524320 | tf_op jit(solution)/shard_map/ppermute | solution.py:225
  26.8 0.7 collective-permute-start.12
  27.5 0.9 shard_map.56
  28.4 0.9 shard_map.57
  29.3 0.4 shard_map.59
  29.7 0.7 collective-permute-start.13
  30.4 0.4 shard_map.62
  30.8 0.7 collective-permute-start.14
  31.5 0.7 collective-permute-start.15
  32.2 0.7 collective-permute-start.16
  32.9 0.9 shard_map.60
  33.8 0.9 shard_map.61
  35.2 0.7 collective-permute-start.17
  36.3 0.7 collective-permute-start.18
  37.0 0.7 collective-permute-start.19
  37.6 0.7 collective-permute-start.20
  38.3 0.9 shard_map.64
  39.2 0.9 shard_map.65
  40.5 0.7 collective-permute-start.21
  41.4 0.7 collective-permute-start.22
  42.1 0.4 shard_map.71
  42.5 0.7 collective-permute-start.23
  43.2 0.7 collective-permute-start.24
  43.9 0.7 collective-permute-start.25
  44.6 0.9 shard_map.68
  45.5 0.9 shard_map.70
  46.7 0.7 collective-permute-start.26
  47.7 0.8 collective-permute-start.27
  48.5 0.4 shard_map.76
  49.0 0.7 collective-permute-start.28
  49.7 0.7 collective-permute-start.29
  50.3 0.7 collective-permute-start.30
  51.0 0.9 shard_map.73
  51.9 0.9 shard_map.75
  53.2 1.3 %collective-permute-start.31 = (bf16[32,2048]{1,0:T(8,128)(2,1)S(1)}, bf16[32,2048]{1,0:T(8,128)(2,1)S(1)}, u32[]{:S(2)}, u32[]{:S(2)}) collective-permute-start(bf16[32,2048]{1,0:T(8,128)(2,1)S(1)} %get-tuple-element.134.refs_2_), channel_id=1, source_target_pairs={{24,28},{25,29},{26,30},{27,31}} | collective-permute-start | bytes 393224 | tf_op jit(solution)/shard_map/ppermute | solution.py:225
  54.7 1.3 %collective-permute-start.32 = (bf16[32,2048]{1,0:T(8,128)(2,1)S(1)}, bf16[32,2048]{1,0:T(8,128)(2,1)S(1)}, u32[]{:S(2)}, u32[]{:S(2)}) collective-permute-start(bf16[32,2048]{1,0:T(8,128)(2,1)S(1)} %get-tuple-element.139.refs_3_), channel_id=1, source_target_pairs={{24,28},{25,29},{26,30},{27,31}} | collective-permute-start | bytes 393224 | tf_op jit(solution)/shard_map/ppermute | solution.py:225
  56.0 0.4 shard_map.81
  56.5 1.3 %collective-permute-start.33 = (f32[32,128]{1,0:T(8,128)S(1)}, f32[32,128]{1,0:T(8,128)S(1)}, u32[]{:S(2)}, u32[]{:S(2)}) collective-permute-start(f32[32,128]{1,0:T(8,128)S(1)} %shard_map.81), channel_id=1, source_target_pairs={{24,29},{25,28},{26,31},{27,30}} | collective-permute-start | bytes 49160 | tf_op jit(solution)/shard_map/ppermute | solution.py:225
  57.8 1.3 %collective-permute-start.34 = (f32[32,128]{1,0:T(8,128)S(1)}, f32[32,128]{1,0:T(8,128)S(1)}, u32[]{:S(2)}, u32[]{:S(2)}) collective-permute-start(f32[32,128]{1,0:T(8,128)S(1)} %shard_map.81), channel_id=1, source_target_pairs={{24,30},{25,31},{26,28},{27,29}} | collective-permute-start | bytes 49160 | tf_op jit(solution)/shard_map/ppermute | solution.py:225
  59.1 1.3 %collective-permute-start.35 = (f32[32,128]{1,0:T(8,128)S(1)}, f32[32,128]{1,0:T(8,128)S(1)}, u32[]{:S(2)}, u32[]{:S(2)}) collective-permute-start(f32[32,128]{1,0:T(8,128)S(1)} %shard_map.81), channel_id=1, source_target_pairs={{24,31},{25,30},{26,29},{27,28}} | collective-permute-start | bytes 49160 | tf_op jit(solution)/shard_map/ppermute | solution.py:225
  60.4 32.1 %collective-permute-done.31.front_ref = bf16[32,2048]{1,0:T(8,128)(2,1)S(1)} collective-permute-done((bf16[32,2048]{1,0:T(8,128)(2,1)S(1)}, bf16[32,2048]{1,0:T(8,128)(2,1)S(1)}, u32[]{:S(2)}, u32[]{:S(2)}) %collective-permute-start.31) | collective-permute-done | bytes 131104 | tf_op jit(solution)/shard_map/ppermute | solution.py:225
  92.5 0.9 shard_map.78
  93.4 1.7 %collective-permute-done.32.front_ref = bf16[32,2048]{1,0:T(8,128)(2,1)S(1)} collective-permute-done((bf16[32,2048]{1,0:T(8,128)(2,1)S(1)}, bf16[32,2048]{1,0:T(8,128)(2,1)S(1)}, u32[]{:S(2)}, u32[]{:S(2)}) %collective-permute-start.32) | collective-permute-done | bytes 131104 | tf_op jit(solution)/shard_map/ppermute | solution.py:225
  95.1 0.9 shard_map.80
  96.1 1.1 %shard_map.82 = (bf16[32,4096]{1,0:T(8,128)(2,1)}, f32[32,128]{1,0:T(8,128)S(1)}) custom-call(f32[32,2048]{1,0:T(8,128)S(1)} %get-tuple-element.135.refs_0_, f32[32,2048]{1,0:T(8,128)S(1)} %get-tuple-element.141.refs_1_, f32[2,32,128]{2,1,0:T(8,128)S(1)} %get-tuple-element.140.refs_0_.refs_2_, ...), custom_call_target="tpu_custom_call", output_to_operand_aliasing={{1}: (4, {})} | custom-call | tf_op jit(solution)/shard_map/pallas_call | solution.py:30
  (55 shorter events, 4.5 us)
Async XLA Ops:
  0.0 6.5 %slice-start = ((s8[8388608]{0:T(1024)(128)(4,1)}), s8[4194304]{0:T(1024)(128)(4,1)S(1)}, s32[]{:S(2)}) async-start(s8[8388608]{0:T(1024)(128)(4,1)} %bitcast.7), calls=%async_computation | async-start | bytes 8388608
  1.5 14.6 %collective-permute-start.4 = (bf16[64,4096]{1,0:T(8,128)(2,1)S(1)}, bf16[64,4096]{1,0:T(8,128)(2,1)S(1)}, u32[]{:S(2)}, u32[]{:S(2)}) collective-permute-start(bf16[64,4096]{1,0:T(8,128)(2,1)S(1)} %bitcast.41), channel_id=1, source_target_pairs={{4,0},{5,1},{6,2},{7,3},{8,4},{9,5},{10,6},{11,7},{12,8},{13,9},{1... | collective-permute-start | bytes 1572872 | tf_op jit(solution)/shard_map/ppermute | solution.py:225
  4.1 2.4 %slice-start.1 = ((s8[8388608]{0:T(1024)(128)(4,1)}), s8[4194304]{0:T(1024)(128)(4,1)S(1)}, s32[]{:S(2)}) async-start(s8[8388608]{0:T(1024)(128)(4,1)} %bitcast.7), calls=%async_computation.1 | async-start | bytes 8388608
  4.1 2.9 %copy-start.1 = (bf16[1,4,64,4096]{3,2,1,0:T(8,128)(2,1)S(1)}, bf16[1,4,64,4096]{3,2,1,0:T(8,128)(2,1)}, u32[]{:S(2)}) copy-start(bf16[1,4,64,4096]{3,2,1,0:T(8,128)(2,1)} %param.6) | copy-start | bytes 6291460
  4.5 4.2 %collective-permute-start = (f32[32,128]{1,0:T(8,128)S(1)}, f32[32,128]{1,0:T(8,128)S(1)}, u32[]{:S(2)}, u32[]{:S(2)}) collective-permute-start(f32[32,128]{1,0:T(8,128)S(1)} %shard_map.48), channel_id=1, source_target_pairs={{0,1},{1,0},{2,3},{3,2},{4,5},{5,4},{6,7},{7,6},{8,9},{9,8},{10,11... | collective-permute-start | bytes 49160 | tf_op jit(solution)/shard_map/ppermute | solution.py:225
  4.6 4.2 %collective-permute-start.1 = (f32[32,128]{1,0:T(8,128)S(1)}, f32[32,128]{1,0:T(8,128)S(1)}, u32[]{:S(2)}, u32[]{:S(2)}) collective-permute-start(f32[32,128]{1,0:T(8,128)S(1)} %shard_map.48), channel_id=1, source_target_pairs={{0,2},{1,3},{2,0},{3,1},{4,6},{5,7},{6,4},{7,5},{8,10},{9,11},{10,... | collective-permute-start | bytes 49160 | tf_op jit(solution)/shard_map/ppermute | solution.py:225
  6.2 3.2 %collective-permute-start.2 = (f32[32,128]{1,0:T(8,128)S(1)}, f32[32,128]{1,0:T(8,128)S(1)}, u32[]{:S(2)}, u32[]{:S(2)}) collective-permute-start(f32[32,128]{1,0:T(8,128)S(1)} %shard_map.48), channel_id=1, source_target_pairs={{0,3},{1,2},{2,1},{3,0},{4,7},{5,6},{6,5},{7,4},{8,11},{9,10},{10,... | collective-permute-start | bytes 49160 | tf_op jit(solution)/shard_map/ppermute | solution.py:225
  6.9 2.4 %copy-start = (bf16[1,4,64,4096]{3,2,1,0:T(8,128)(2,1)S(1)}, bf16[1,4,64,4096]{3,2,1,0:T(8,128)(2,1)}, u32[]{:S(2)}) copy-start(bf16[1,4,64,4096]{3,2,1,0:T(8,128)(2,1)} %param.7) | copy-start | bytes 6291460
  9.7 7.9 %collective-permute-start.3 = (bf16[32,4096]{1,0:T(8,128)(2,1)S(1)}, bf16[32,4096]{1,0:T(8,128)(2,1)S(1)}, u32[]{:S(2)}, u32[]{:S(2)}) collective-permute-start(bf16[32,4096]{1,0:T(8,128)(2,1)S(1)} %get-tuple-element.83.refs_1_), channel_id=1, source_target_pairs={{0,4},{1,5},{2,6},{3,7}} | collective-permute-start | bytes 786440 | tf_op jit(solution)/shard_map/ppermute | solution.py:225
  10.4 16.0 %collective-permute-start.11 = (bf16[64,4096]{1,0:T(8,128)(2,1)S(1)}, bf16[64,4096]{1,0:T(8,128)(2,1)S(1)}, u32[]{:S(2)}, u32[]{:S(2)}) collective-permute-start(bf16[64,4096]{1,0:T(8,128)(2,1)S(1)} %bitcast.38), channel_id=1, source_target_pairs={{12,8},{13,9},{14,10},{15,11},{16,12},{17,13},{18,14},{19,15},{20,... | collective-permute-start | bytes 1572872 | tf_op jit(solution)/shard_map/ppermute | solution.py:225
  16.3 2.4 %collective-permute-start.5 = (f32[32,128]{1,0:T(8,128)S(1)}, f32[32,128]{1,0:T(8,128)S(1)}, u32[]{:S(2)}, u32[]{:S(2)}) collective-permute-start(f32[32,128]{1,0:T(8,128)S(1)} %shard_map.50.refs_0_), channel_id=1, source_target_pairs={{0,6},{1,7},{2,4},{3,5}} | collective-permute-start | bytes 49160 | tf_op jit(solution)/shard_map/ppermute | solution.py:225
  17.0 1.7 %collective-permute-start.6 = (f32[32,128]{1,0:T(8,128)S(1)}, f32[32,128]{1,0:T(8,128)S(1)}, u32[]{:S(2)}, u32[]{:S(2)}) collective-permute-start(f32[32,128]{1,0:T(8,128)S(1)} %shard_map.50.refs_0_), channel_id=1, source_target_pairs={{0,7},{1,6},{2,5},{3,4}} | collective-permute-start | bytes 49160 | tf_op jit(solution)/shard_map/ppermute | solution.py:225
  18.0 2.5 %collective-permute-start.7 = (f32[32,128]{1,0:T(8,128)S(1)}, f32[32,128]{1,0:T(8,128)S(1)}, u32[]{:S(2)}, u32[]{:S(2)}) collective-permute-start(f32[32,128]{1,0:T(8,128)S(1)} %shard_map.53), channel_id=1, source_target_pairs={{4,5},{5,4},{6,7},{7,6}} | collective-permute-start | bytes 49160 | tf_op jit(solution)/shard_map/ppermute | solution.py:225
  21.0 5.5 %collective-permute-start.8 = (bf16[32,4096]{1,0:T(8,128)(2,1)S(1)}, bf16[32,4096]{1,0:T(8,128)(2,1)S(1)}, u32[]{:S(2)}, u32[]{:S(2)}) collective-permute-start(bf16[32,4096]{1,0:T(8,128)(2,1)S(1)} %get-tuple-element.91.refs_1_), channel_id=1, source_target_pairs={{4,8},{5,9},{6,10},{7,11}} | collective-permute-start | bytes 786440 | tf_op jit(solution)/shard_map/ppermute | solution.py:225
  21.9 5.5 %collective-permute-start.10 = (f32[32,128]{1,0:T(8,128)S(1)}, f32[32,128]{1,0:T(8,128)S(1)}, u32[]{:S(2)}, u32[]{:S(2)}) collective-permute-start(f32[32,128]{1,0:T(8,128)S(1)} %shard_map.55), channel_id=1, source_target_pairs={{4,11},{5,10},{6,9},{7,8}} | collective-permute-start | bytes 49160 | tf_op jit(solution)/shard_map/ppermute | solution.py:225
  22.6 4.9 %collective-permute-start.9 = (f32[32,128]{1,0:T(8,128)S(1)}, f32[32,128]{1,0:T(8,128)S(1)}, u32[]{:S(2)}, u32[]{:S(2)}) collective-permute-start(f32[32,128]{1,0:T(8,128)S(1)} %shard_map.55), channel_id=1, source_target_pairs={{4,10},{5,11},{6,8},{7,9}} | collective-permute-start | bytes 49160 | tf_op jit(solution)/shard_map/ppermute | solution.py:225
  26.8 2.5 %collective-permute-start.12 = (f32[32,128]{1,0:T(8,128)S(1)}, f32[32,128]{1,0:T(8,128)S(1)}, u32[]{:S(2)}, u32[]{:S(2)}) collective-permute-start(f32[32,128]{1,0:T(8,128)S(1)} %shard_map.58), channel_id=1, source_target_pairs={{8,9},{9,8},{10,11},{11,10}} | collective-permute-start | bytes 49160 | tf_op jit(solution)/shard_map/ppermute | solution.py:225
  29.7 3.2 %collective-permute-start.13 = (bf16[32,4096]{1,0:T(8,128)(2,1)S(1)}, bf16[32,4096]{1,0:T(8,128)(2,1)S(1)}, u32[]{:S(2)}, u32[]{:S(2)}) collective-permute-start(bf16[32,4096]{1,0:T(8,128)(2,1)S(1)} %get-tuple-element.99.refs_2_), channel_id=1, source_target_pairs={{8,12},{9,13},{10,14},{11,15}} | collective-permute-start | bytes 786440 | tf_op jit(solution)/shard_map/ppermute | solution.py:225
  30.8 3.9 %collective-permute-start.14 = (f32[32,128]{1,0:T(8,128)S(1)}, f32[32,128]{1,0:T(8,128)S(1)}, u32[]{:S(2)}, u32[]{:S(2)}) collective-permute-start(f32[32,128]{1,0:T(8,128)S(1)} %shard_map.62), channel_id=1, source_target_pairs={{8,13},{9,12},{10,15},{11,14}} | collective-permute-start | bytes 49160 | tf_op jit(solution)/shard_map/ppermute | solution.py:225
  31.5 3.2 %collective-permute-start.15 = (f32[32,128]{1,0:T(8,128)S(1)}, f32[32,128]{1,0:T(8,128)S(1)}, u32[]{:S(2)}, u32[]{:S(2)}) collective-permute-start(f32[32,128]{1,0:T(8,128)S(1)} %shard_map.62), channel_id=1, source_target_pairs={{8,14},{9,15},{10,12},{11,13}} | collective-permute-start | bytes 49160 | tf_op jit(solution)/shard_map/ppermute | solution.py:225
  32.2 2.5 %collective-permute-start.16 = (f32[32,128]{1,0:T(8,128)S(1)}, f32[32,128]{1,0:T(8,128)S(1)}, u32[]{:S(2)}, u32[]{:S(2)}) collective-permute-start(f32[32,128]{1,0:T(8,128)S(1)} %shard_map.62), channel_id=1, source_target_pairs={{8,15},{9,14},{10,13},{11,12}} | collective-permute-start | bytes 49160 | tf_op jit(solution)/shard_map/ppermute | solution.py:225
  35.2 3.2 %collective-permute-start.17 = (bf16[32,4096]{1,0:T(8,128)(2,1)S(1)}, bf16[32,4096]{1,0:T(8,128)(2,1)S(1)}, u32[]{:S(2)}, u32[]{:S(2)}) collective-permute-start(bf16[32,4096]{1,0:T(8,128)(2,1)S(1)} %get-tuple-element.107.refs_2_), channel_id=1, source_target_pairs={{12,16},{13,17},{14,18},{15,19}} | collective-permute-start | bytes 786440 | tf_op jit(solution)/shard_map/ppermute | solution.py:225
  36.3 3.9 %collective-permute-start.18 = (f32[32,128]{1,0:T(8,128)S(1)}, f32[32,128]{1,0:T(8,128)S(1)}, u32[]{:S(2)}, u32[]{:S(2)}) collective-permute-start(f32[32,128]{1,0:T(8,128)S(1)} %shard_map.66), channel_id=1, source_target_pairs={{12,17},{13,16},{14,19},{15,18}} | collective-permute-start | bytes 49160 | tf_op jit(solution)/shard_map/ppermute | solution.py:225
  37.0 3.2 %collective-permute-start.19 = (f32[32,128]{1,0:T(8,128)S(1)}, f32[32,128]{1,0:T(8,128)S(1)}, u32[]{:S(2)}, u32[]{:S(2)}) collective-permute-start(f32[32,128]{1,0:T(8,128)S(1)} %shard_map.66), channel_id=1, source_target_pairs={{12,18},{13,19},{14,16},{15,17}} | collective-permute-start | bytes 49160 | tf_op jit(solution)/shard_map/ppermute | solution.py:225
  37.6 2.5 %collective-permute-start.20 = (f32[32,128]{1,0:T(8,128)S(1)}, f32[32,128]{1,0:T(8,128)S(1)}, u32[]{:S(2)}, u32[]{:S(2)}) collective-permute-start(f32[32,128]{1,0:T(8,128)S(1)} %shard_map.66), channel_id=1, source_target_pairs={{12,19},{13,18},{14,17},{15,16}} | collective-permute-start | bytes 49160 | tf_op jit(solution)/shard_map/ppermute | solution.py:225
  40.5 4.1 %collective-permute-start.21 = (bf16[32,2048]{1,0:T(8,128)(2,1)S(1)}, bf16[32,2048]{1,0:T(8,128)(2,1)S(1)}, u32[]{:S(2)}, u32[]{:S(2)}) collective-permute-start(bf16[32,2048]{1,0:T(8,128)(2,1)S(1)} %get-tuple-element.114.refs_2_), channel_id=1, source_target_pairs={{16,20},{17,21},{18,22},{19,23}} | collective-permute-start | bytes 393224 | tf_op jit(solution)/shard_map/ppermute | solution.py:225
  41.4 4.1 %collective-permute-start.22 = (bf16[32,2048]{1,0:T(8,128)(2,1)S(1)}, bf16[32,2048]{1,0:T(8,128)(2,1)S(1)}, u32[]{:S(2)}, u32[]{:S(2)}) collective-permute-start(bf16[32,2048]{1,0:T(8,128)(2,1)S(1)} %get-tuple-element.121.refs_3_), channel_id=1, source_target_pairs={{16,20},{17,21},{18,22},{19,23}} | collective-permute-start | bytes 393224 | tf_op jit(solution)/shard_map/ppermute | solution.py:225
  42.5 3.9 %collective-permute-start.23 = (f32[32,128]{1,0:T(8,128)S(1)}, f32[32,128]{1,0:T(8,128)S(1)}, u32[]{:S(2)}, u32[]{:S(2)}) collective-permute-start(f32[32,128]{1,0:T(8,128)S(1)} %shard_map.71), channel_id=1, source_target_pairs={{16,21},{17,20},{18,23},{19,22}} | collective-permute-start | bytes 49160 | tf_op jit(solution)/shard_map/ppermute | solution.py:225
  43.2 3.2 %collective-permute-start.24 = (f32[32,128]{1,0:T(8,128)S(1)}, f32[32,128]{1,0:T(8,128)S(1)}, u32[]{:S(2)}, u32[]{:S(2)}) collective-permute-start(f32[32,128]{1,0:T(8,128)S(1)} %shard_map.71), channel_id=1, source_target_pairs={{16,22},{17,23},{18,20},{19,21}} | collective-permute-start | bytes 49160 | tf_op jit(solution)/shard_map/ppermute | solution.py:225
  43.9 2.5 %collective-permute-start.25 = (f32[32,128]{1,0:T(8,128)S(1)}, f32[32,128]{1,0:T(8,128)S(1)}, u32[]{:S(2)}, u32[]{:S(2)}) collective-permute-start(f32[32,128]{1,0:T(8,128)S(1)} %shard_map.71), channel_id=1, source_target_pairs={{16,23},{17,22},{18,21},{19,20}} | collective-permute-start | bytes 49160 | tf_op jit(solution)/shard_map/ppermute | solution.py:225
  46.7 4.3 %collective-permute-start.26 = (bf16[32,2048]{1,0:T(8,128)(2,1)S(1)}, bf16[32,2048]{1,0:T(8,128)(2,1)S(1)}, u32[]{:S(2)}, u32[]{:S(2)}) collective-permute-start(bf16[32,2048]{1,0:T(8,128)(2,1)S(1)} %get-tuple-element.124.refs_2_), channel_id=1, source_target_pairs={{20,24},{21,25},{22,26},{23,27}} | collective-permute-start | bytes 393224 | tf_op jit(solution)/shard_map/ppermute | solution.py:225
  47.7 4.3 %collective-permute-start.27 = (bf16[32,2048]{1,0:T(8,128)(2,1)S(1)}, bf16[32,2048]{1,0:T(8,128)(2,1)S(1)}, u32[]{:S(2)}, u32[]{:S(2)}) collective-permute-start(bf16[32,2048]{1,0:T(8,128)(2,1)S(1)} %get-tuple-element.131.refs_3_), channel_id=1, source_target_pairs={{20,24},{21,25},{22,26},{23,27}} | collective-permute-start | bytes 393224 | tf_op jit(solution)/shard_map/ppermute | solution.py:225
  49.0 3.9 %collective-permute-start.28 = (f32[32,128]{1,0:T(8,128)S(1)}, f32[32,128]{1,0:T(8,128)S(1)}, u32[]{:S(2)}, u32[]{:S(2)}) collective-permute-start(f32[32,128]{1,0:T(8,128)S(1)} %shard_map.76), channel_id=1, source_target_pairs={{20,25},{21,24},{22,27},{23,26}} | collective-permute-start | bytes 49160 | tf_op jit(solution)/shard_map/ppermute | solution.py:225
  49.7 3.2 %collective-permute-start.29 = (f32[32,128]{1,0:T(8,128)S(1)}, f32[32,128]{1,0:T(8,128)S(1)}, u32[]{:S(2)}, u32[]{:S(2)}) collective-permute-start(f32[32,128]{1,0:T(8,128)S(1)} %shard_map.76), channel_id=1, source_target_pairs={{20,26},{21,27},{22,24},{23,25}} | collective-permute-start | bytes 49160 | tf_op jit(solution)/shard_map/ppermute | solution.py:225
  50.3 2.5 %collective-permute-start.30 = (f32[32,128]{1,0:T(8,128)S(1)}, f32[32,128]{1,0:T(8,128)S(1)}, u32[]{:S(2)}, u32[]{:S(2)}) collective-permute-start(f32[32,128]{1,0:T(8,128)S(1)} %shard_map.76), channel_id=1, source_target_pairs={{20,27},{21,26},{22,25},{23,24}} | collective-permute-start | bytes 49160 | tf_op jit(solution)/shard_map/ppermute | solution.py:225
  53.2 39.4 %collective-permute-start.31 = (bf16[32,2048]{1,0:T(8,128)(2,1)S(1)}, bf16[32,2048]{1,0:T(8,128)(2,1)S(1)}, u32[]{:S(2)}, u32[]{:S(2)}) collective-permute-start(bf16[32,2048]{1,0:T(8,128)(2,1)S(1)} %get-tuple-element.134.refs_2_), channel_id=1, source_target_pairs={{24,28},{25,29},{26,30},{27,31}} | collective-permute-start | bytes 393224 | tf_op jit(solution)/shard_map/ppermute | solution.py:225
  54.7 40.4 %collective-permute-start.32 = (bf16[32,2048]{1,0:T(8,128)(2,1)S(1)}, bf16[32,2048]{1,0:T(8,128)(2,1)S(1)}, u32[]{:S(2)}, u32[]{:S(2)}) collective-permute-start(bf16[32,2048]{1,0:T(8,128)(2,1)S(1)} %get-tuple-element.139.refs_3_), channel_id=1, source_target_pairs={{24,28},{25,29},{26,30},{27,31}} | collective-permute-start | bytes 393224 | tf_op jit(solution)/shard_map/ppermute | solution.py:225
  56.5 39.6 %collective-permute-start.33 = (f32[32,128]{1,0:T(8,128)S(1)}, f32[32,128]{1,0:T(8,128)S(1)}, u32[]{:S(2)}, u32[]{:S(2)}) collective-permute-start(f32[32,128]{1,0:T(8,128)S(1)} %shard_map.81), channel_id=1, source_target_pairs={{24,29},{25,28},{26,31},{27,30}} | collective-permute-start | bytes 49160 | tf_op jit(solution)/shard_map/ppermute | solution.py:225
  57.8 38.2 %collective-permute-start.34 = (f32[32,128]{1,0:T(8,128)S(1)}, f32[32,128]{1,0:T(8,128)S(1)}, u32[]{:S(2)}, u32[]{:S(2)}) collective-permute-start(f32[32,128]{1,0:T(8,128)S(1)} %shard_map.81), channel_id=1, source_target_pairs={{24,30},{25,31},{26,28},{27,29}} | collective-permute-start | bytes 49160 | tf_op jit(solution)/shard_map/ppermute | solution.py:225
  59.1 36.9 %collective-permute-start.35 = (f32[32,128]{1,0:T(8,128)S(1)}, f32[32,128]{1,0:T(8,128)S(1)}, u32[]{:S(2)}, u32[]{:S(2)}) collective-permute-start(f32[32,128]{1,0:T(8,128)S(1)} %shard_map.81), channel_id=1, source_target_pairs={{24,31},{25,30},{26,29},{27,28}} | collective-permute-start | bytes 49160 | tf_op jit(solution)/shard_map/ppermute | solution.py:225
where the time goes:
time: 98 us; the launch traced here: 97.2 us
  waiting for transfers between devices  40 us (41%)
  starting transfers between devices  32 us (33%)
  Pallas kernels  24 us (24%)
    ppermute x36, waiting for transfers between devices, moved(): return lax.ppermute(x, ('slab', 'hodlr'), route)  40 us
    ppermute x36, starting transfers between devices, moved(): return lax.ppermute(x, ('slab', 'hodlr'), route)  32 us
    pallas_call x37, Pallas kernels, call(): pl.pallas_call(kernel, out_shape=outs, in_specs=[remote if i in from_hbm...  24 us
  transfers between devices with their start and end apart: 36, of which 5 were waited for; matrix products, arithmetic and copies ran while one was open for 0% of the time, Pallas kernels for 20%

commit v1 on v0

--- a/solution.py
+++ b/solution.py
@@ -9,7 +9,6 @@
 
 VMEM_LIMIT = 24 * 1024 * 1024
 FIRST_SHARE = 2
-SPLIT_HOPS = 3
 IN_PLACE = 2
 OPEN_FLOPS = 4 * 10**9
 ROWS_TIMES_COLUMNS = (((1,), (0,)), ((), ()))
@@ -99,12 +98,13 @@
     w_refs, (leaf_ref, v_ref), near_out = refs[:n], refs[n : n + 2], refs[n + 2]
     sum_refs, p_refs = refs[n + 3 : 2 * n + 3], refs[2 * n + 3 :]
     size = leaf_ref.shape[1]
-    near = near_out.shape[1]
+    near = p_refs[0].shape[2]
     for i, span in enumerate(spans):
         for j, c in enumerate(leaves_of(span, size)):
             columns = slice(j * size, (j + 1) * size)
             turned = v_ref[cross:, :, c * size : (c + 1) * size].reshape(near, size).T
-            near_out[c * size : (c + 1) * size, :] = turned
+            group = near_out.shape[2] // near
+            near_out[c // group, :, c % group * near : (c % group + 1) * near] = turned
             p_refs[i][j] = dot(w_refs[i][:, columns], turned)
             sum_refs[i][:, columns] = dot(w_refs[i][:, columns], leaf_ref[c])
 
@@ -114,7 +114,8 @@
     size = leaf.shape[1]
     rows = w[0].shape[0]
     near = (levels - cross) * rank
-    outs = [pltpu.VMEM((width, near), v.dtype)]
+    group = 2 if all((stop - start) // size % 2 == 0 for start, stop in spans) else 1
+    outs = [pltpu.VMEM((width // size // group, size, group * near), v.dtype)]
     outs += [pltpu.VMEM(x.shape, jnp.float32) for x in w]
     outs += [pltpu.VMEM((x.shape[1] // size, rows, near), jnp.float32) for x in w]
     n = len(w)
@@ -139,19 +140,28 @@
 def near_kernel(span, start, w_ref, front_ref, leaf_ref, v_ref, *refs):
     w_out, sum_out, p_out = refs[-3:]
     size = leaf_ref.shape[1]
+    rows = w_ref.shape[0]
+    near = p_out.shape[2]
+    group = v_ref.shape[2] // near
+    members = []
     for j, c in enumerate(leaves_of(span, size)):
         columns = slice(j * size, (j + 1) * size)
         w = w_ref[:, columns] + front_ref[:, start + j * size : start + (j + 1) * size]
         w_out[:, columns] = w
-        p_out[j] = dot(w, v_ref[c * size : (c + 1) * size, :])
+        members.append(w)
+        if len(members) == group:
+            both = dot(jnp.concatenate(members, axis=0), v_ref[c // group])
+            for i in range(group):
+                p_out[j - group + 1 + i] = both[i * rows : (i + 1) * rows, i * near : (i + 1) * near]
+            members = []
         sum_out[:, columns] = dot(w, leaf_ref[c])
 
 
-def near_part(span, start, w, front, leaf, near_v, behind):
+def near_part(span, start, near, w, front, leaf, near_v, behind):
     outs = [
         pltpu.VMEM(w.shape, w.dtype),
         pltpu.VMEM(w.shape, jnp.float32),
-        pltpu.VMEM((w.shape[1] // leaf.shape[1], w.shape[0], near_v.shape[1]), jnp.float32),
+        pltpu.VMEM((w.shape[1] // leaf.shape[1], w.shape[0], near), jnp.float32),
     ]
     return call(functools.partial(near_kernel, span, start), outs, [w, front, leaf, near_v, *behind], {0: 0})
 
@@ -255,11 +265,11 @@
         for i, span in enumerate(spans):
             behind = projected[i - 1 : i] if i else first
             given, start = (front[0], span[0]) if len(front) == 1 else (front[i], 0)
-            w[i], sums[i], projected[i] = near_part(span, start, w[i], given, leaf, near_v, behind)
+            w[i], sums[i], projected[i] = near_part(span, start, (levels - cross) * rank, w[i], given, leaf, near_v, behind)
         if k == chain - 1:
             out, _ = far(every, sums, projected, q, parts, levels_of, u, True)
             return out[None]
-        split = k >= chain - 1 - SPLIT_HOPS
+        split = k >= IN_PLACE and k % 2 == 0
         outs, front = [], []
         for chosen in [(i,) for i in every] if split else [every]:
             out, q = far(chosen, sums, projected, q, [] if front else parts, levels_of, u, False)

time: 98 us -> 98.1 us (level)
  transfers between devices with their start and end apart: 36 -> 36, of which waited for: 5 -> 6; matrix products, arithmetic and copies ran while one was open for 0% -> 0% of each run, Pallas kernels for 20% -> 20%
where the time goes in v1:
time: 98.1 us; the launch traced here: 97.3 us
  waiting for transfers between devices  40.2 us (41%)
  starting transfers between devices  32 us (33%)
  Pallas kernels  23.9 us (24%)
    ppermute x36, waiting for transfers between devices, moved(): return lax.ppermute(x, ('slab', 'hodlr'), route)  40.2 us
    ppermute x36, starting transfers between devices, moved(): return lax.ppermute(x, ('slab', 'hodlr'), route)  32 us
    pallas_call x37, Pallas kernels, call(): pl.pallas_call(kernel, out_shape=outs, in_specs=[remote if i in from_hbm...  23.9 us
  transfers between devices with their start and end apart: 36, of which 6 were waited for; matrix products, arithmetic and copies ran while one was open for 0% of the time, Pallas kernels for 20%

profile of v1, /device:TPU:26, one launch (start us, length us, event | category | flops | bytes accessed | tf_op | source)
XLA Modules:
  0.0 97.3 jit_solution(15755439956058937447)
XLA Ops:
  0.0 1.4 %shard_map.46 = (bf16[1,64,4096]{2,1,0:T(8,128)(2,1)S(1)}, bf16[1,64,4096]{2,1,0:T(8,128)(2,1)S(1)}, bf16[32,2048]{1,0:T(8,128)(2,1)S(1)}, bf16[32,2048]{1,0:T(8,128)(2,1)S(1)}) custom-call(bf16[32,4096]{1,0:T(8,128)(2,1)} %bitcast.43, bf16[4,64,4096]{2,1,0:T(8,128)(2,1)} %bitcast.35), custom_call_target="tpu_custom_call" | custom-call | tf_op jit(solution)/shard_map/pallas_call | solution.py:29
  1.5 2.6 %collective-permute-start.4 = (bf16[64,4096]{1,0:T(8,128)(2,1)S(1)}, bf16[64,4096]{1,0:T(8,128)(2,1)S(1)}, u32[]{:S(2)}, u32[]{:S(2)}) collective-permute-start(bf16[64,4096]{1,0:T(8,128)(2,1)S(1)} %bitcast.41), channel_id=1, source_target_pairs={{4,0},{5,1},{6,2},{7,3},{8,4},{9,5},{10,6},{11,7},{12,8},{13,9},{1... | collective-permute-start | bytes 1572872 | tf_op jit(solution)/shard_map/ppermute | solution.py:235
  4.1 0.4 shard_map.48
  4.6 1.6 %collective-permute-start.1 = (f32[32,128]{1,0:T(8,128)S(1)}, f32[32,128]{1,0:T(8,128)S(1)}, u32[]{:S(2)}, u32[]{:S(2)}) collective-permute-start(f32[32,128]{1,0:T(8,128)S(1)} %shard_map.48), channel_id=1, source_target_pairs={{0,2},{1,3},{2,0},{3,1},{4,6},{5,7},{6,4},{7,5},{8,10},{9,11},{10,... | collective-permute-start | bytes 49160 | tf_op jit(solution)/shard_map/ppermute | solution.py:235
  6.5 0.5 copy-done.1
  6.9 1.8 %shard_map.47 = (bf16[2,1024,256]{2,1,0:T(8,128)(2,1)S(1)}, f32[32,2048]{1,0:T(8,128)S(1)}, f32[32,2048]{1,0:T(8,128)S(1)}, f32[2,32,128]{2,1,0:T(8,128)S(1)}, f32[2,32,128]{2,1,0:T(8,128)S(1)}) custom-call(bf16[32,2048]{1,0:T(8,128)(2,1)S(1)} %get-tuple-element.75.refs_0_.refs_2_.w_ref, bf16[32,2048]{1,0:T(8,128)(2,1)S(1)} %get-tuple-element.76.refs_1_.refs_3_.w_ref, ...), custom_call_target="tpu_custom_call" | custom-call | tf_op jit(solution)/shard_map/pallas_call | solution.py:29
  8.8 0.6 collective-permute-done.2.refs_7_
  9.7 0.7 collective-permute-start.3
  10.4 3.3 %collective-permute-start.11 = (bf16[64,4096]{1,0:T(8,128)(2,1)S(1)}, bf16[64,4096]{1,0:T(8,128)(2,1)S(1)}, u32[]{:S(2)}, u32[]{:S(2)}) collective-permute-start(bf16[64,4096]{1,0:T(8,128)(2,1)S(1)} %bitcast.38), channel_id=1, source_target_pairs={{12,8},{13,9},{14,10},{15,11},{16,12},{17,13},{18,14},{19,15},{20,... | collective-permute-start | bytes 1572872 | tf_op jit(solution)/shard_map/ppermute | solution.py:235
  13.7 2.3 %collective-permute-done.4.refs_0_ = bf16[64,4096]{1,0:T(8,128)(2,1)S(1)} collective-permute-done((bf16[64,4096]{1,0:T(8,128)(2,1)S(1)}, bf16[64,4096]{1,0:T(8,128)(2,1)S(1)}, u32[]{:S(2)}, u32[]{:S(2)}) %collective-permute-start.4) | collective-permute-done | bytes 524320 | tf_op jit(solution)/shard_map/ppermute | solution.py:235
  16.3 0.7 collective-permute-start.5
  17.0 0.7 collective-permute-start.6
  18.0 0.7 collective-permute-start.7
  18.7 0.9 shard_map.51
  19.6 0.9 shard_map.52
  20.9 0.7 collective-permute-start.8
  21.9 0.7 collective-permute-start.10
  22.6 0.7 collective-permute-start.9
  23.2 3.2 %collective-permute-done.11.refs_0_.refs_1_ = bf16[64,4096]{1,0:T(8,128)(2,1)S(1)} collective-permute-done((bf16[64,4096]{1,0:T(8,128)(2,1)S(1)}, bf16[64,4096]{1,0:T(8,128)(2,1)S(1)}, u32[]{:S(2)}, u32[]{:S(2)}) %collective-permute-start.11) | collective-permute-done | bytes 524320 | tf_op jit(solution)/shard_map/ppermute | solution.py:235
  26.8 0.7 collective-permute-start.12
  27.5 0.9 shard_map.56
  28.4 0.9 shard_map.57
  29.6 0.7 collective-permute-start.13
  30.5 0.7 collective-permute-start.14
  31.2 0.4 shard_map.63
  31.6 0.7 collective-permute-start.15
  32.3 0.7 collective-permute-start.16
  33.0 0.7 collective-permute-start.17
  33.7 0.9 shard_map.60
  34.6 0.9 shard_map.62
  35.9 0.7 collective-permute-start.18
  36.6 0.4 shard_map.67
  37.0 0.7 collective-permute-start.19
  37.8 0.7 collective-permute-start.20
  38.4 0.7 collective-permute-start.21
  39.1 0.9 shard_map.65
  40.0 0.9 shard_map.66
  41.2 0.7 collective-permute-start.22
  42.2 0.7 collective-permute-start.23
  42.9 0.4 shard_map.72
  43.3 0.7 collective-permute-start.24
  44.0 0.7 collective-permute-start.25
  44.7 0.8 collective-permute-start.26
  45.5 0.9 shard_map.69
  46.5 0.9 shard_map.71
  47.8 0.7 collective-permute-start.27
  48.5 0.4 shard_map.76
  48.9 0.7 collective-permute-start.28
  49.6 0.7 collective-permute-start.29
  50.3 0.7 collective-permute-start.30
  51.0 0.9 shard_map.74
  51.9 0.9 shard_map.75
  53.1 1.3 %collective-permute-start.31 = (bf16[32,2048]{1,0:T(8,128)(2,1)S(1)}, bf16[32,2048]{1,0:T(8,128)(2,1)S(1)}, u32[]{:S(2)}, u32[]{:S(2)}) collective-permute-start(bf16[32,2048]{1,0:T(8,128)(2,1)S(1)} %get-tuple-element.134.refs_2_), channel_id=1, source_target_pairs={{24,28},{25,29},{26,30},{27,31}} | collective-permute-start | bytes 393224 | tf_op jit(solution)/shard_map/ppermute | solution.py:235
  54.7 1.3 %collective-permute-start.32 = (bf16[32,2048]{1,0:T(8,128)(2,1)S(1)}, bf16[32,2048]{1,0:T(8,128)(2,1)S(1)}, u32[]{:S(2)}, u32[]{:S(2)}) collective-permute-start(bf16[32,2048]{1,0:T(8,128)(2,1)S(1)} %get-tuple-element.139.refs_3_), channel_id=1, source_target_pairs={{24,28},{25,29},{26,30},{27,31}} | collective-permute-start | bytes 393224 | tf_op jit(solution)/shard_map/ppermute | solution.py:235
  56.0 0.4 shard_map.81
  56.4 1.3 %collective-permute-start.33 = (f32[32,128]{1,0:T(8,128)S(1)}, f32[32,128]{1,0:T(8,128)S(1)}, u32[]{:S(2)}, u32[]{:S(2)}) collective-permute-start(f32[32,128]{1,0:T(8,128)S(1)} %shard_map.81), channel_id=1, source_target_pairs={{24,29},{25,28},{26,31},{27,30}} | collective-permute-start | bytes 49160 | tf_op jit(solution)/shard_map/ppermute | solution.py:235
  57.7 1.3 %collective-permute-start.34 = (f32[32,128]{1,0:T(8,128)S(1)}, f32[32,128]{1,0:T(8,128)S(1)}, u32[]{:S(2)}, u32[]{:S(2)}) collective-permute-start(f32[32,128]{1,0:T(8,128)S(1)} %shard_map.81), channel_id=1, source_target_pairs={{24,30},{25,31},{26,28},{27,29}} | collective-permute-start | bytes 49160 | tf_op jit(solution)/shard_map/ppermute | solution.py:235
  59.0 1.3 %collective-permute-start.35 = (f32[32,128]{1,0:T(8,128)S(1)}, f32[32,128]{1,0:T(8,128)S(1)}, u32[]{:S(2)}, u32[]{:S(2)}) collective-permute-start(f32[32,128]{1,0:T(8,128)S(1)} %shard_map.81), channel_id=1, source_target_pairs={{24,31},{25,30},{26,29},{27,28}} | collective-permute-start | bytes 49160 | tf_op jit(solution)/shard_map/ppermute | solution.py:235
  60.3 32.3 %collective-permute-done.31.front_ref = bf16[32,2048]{1,0:T(8,128)(2,1)S(1)} collective-permute-done((bf16[32,2048]{1,0:T(8,128)(2,1)S(1)}, bf16[32,2048]{1,0:T(8,128)(2,1)S(1)}, u32[]{:S(2)}, u32[]{:S(2)}) %collective-permute-start.31) | collective-permute-done | bytes 131104 | tf_op jit(solution)/shard_map/ppermute | solution.py:235
  92.7 0.9 shard_map.78
  93.6 1.0 %collective-permute-done.32.front_ref = bf16[32,2048]{1,0:T(8,128)(2,1)S(1)} collective-permute-done((bf16[32,2048]{1,0:T(8,128)(2,1)S(1)}, bf16[32,2048]{1,0:T(8,128)(2,1)S(1)}, u32[]{:S(2)}, u32[]{:S(2)}) %collective-permute-start.32) | collective-permute-done | bytes 131104 | tf_op jit(solution)/shard_map/ppermute | solution.py:235
  94.6 0.9 shard_map.80
  95.5 0.7 collective-permute-done.34.refs_6_
  96.2 1.1 %shard_map.82 = (bf16[32,4096]{1,0:T(8,128)(2,1)}, f32[32,128]{1,0:T(8,128)S(1)}) custom-call(f32[32,2048]{1,0:T(8,128)S(1)} %get-tuple-element.135.refs_0_, f32[32,2048]{1,0:T(8,128)S(1)} %get-tuple-element.141.refs_1_, f32[2,32,128]{2,1,0:T(8,128)S(1)} %get-tuple-element.140.refs_0_.refs_2_, ...), custom_call_target="tpu_custom_call", output_to_operand_aliasing={{1}: (4, {})} | custom-call | tf_op jit(solution)/shard_map/pallas_call | solution.py:29
  (55 shorter events, 4.8 us)
Async XLA Ops:
  0.0 6.5 %slice-start = ((s8[8388608]{0:T(1024)(128)(4,1)}), s8[4194304]{0:T(1024)(128)(4,1)S(1)}, s32[]{:S(2)}) async-start(s8[8388608]{0:T(1024)(128)(4,1)} %bitcast.7), calls=%async_computation | async-start | bytes 8388608
  1.5 14.6 %collective-permute-start.4 = (bf16[64,4096]{1,0:T(8,128)(2,1)S(1)}, bf16[64,4096]{1,0:T(8,128)(2,1)S(1)}, u32[]{:S(2)}, u32[]{:S(2)}) collective-permute-start(bf16[64,4096]{1,0:T(8,128)(2,1)S(1)} %bitcast.41), channel_id=1, source_target_pairs={{4,0},{5,1},{6,2},{7,3},{8,4},{9,5},{10,6},{11,7},{12,8},{13,9},{1... | collective-permute-start | bytes 1572872 | tf_op jit(solution)/shard_map/ppermute | solution.py:235
  4.1 2.4 %slice-start.1 = ((s8[8388608]{0:T(1024)(128)(4,1)}), s8[4194304]{0:T(1024)(128)(4,1)S(1)}, s32[]{:S(2)}) async-start(s8[8388608]{0:T(1024)(128)(4,1)} %bitcast.7), calls=%async_computation.1 | async-start | bytes 8388608
  4.1 2.9 %copy-start.1 = (bf16[1,4,64,4096]{3,2,1,0:T(8,128)(2,1)S(1)}, bf16[1,4,64,4096]{3,2,1,0:T(8,128)(2,1)}, u32[]{:S(2)}) copy-start(bf16[1,4,64,4096]{3,2,1,0:T(8,128)(2,1)} %param.6) | copy-start | bytes 6291460
  4.5 4.2 %collective-permute-start = (f32[32,128]{1,0:T(8,128)S(1)}, f32[32,128]{1,0:T(8,128)S(1)}, u32[]{:S(2)}, u32[]{:S(2)}) collective-permute-start(f32[32,128]{1,0:T(8,128)S(1)} %shard_map.48), channel_id=1, source_target_pairs={{0,1},{1,0},{2,3},{3,2},{4,5},{5,4},{6,7},{7,6},{8,9},{9,8},{10,11... | collective-permute-start | bytes 49160 | tf_op jit(solution)/shard_map/ppermute | solution.py:235
  4.6 4.2 %collective-permute-start.1 = (f32[32,128]{1,0:T(8,128)S(1)}, f32[32,128]{1,0:T(8,128)S(1)}, u32[]{:S(2)}, u32[]{:S(2)}) collective-permute-start(f32[32,128]{1,0:T(8,128)S(1)} %shard_map.48), channel_id=1, source_target_pairs={{0,2},{1,3},{2,0},{3,1},{4,6},{5,7},{6,4},{7,5},{8,10},{9,11},{10,... | collective-permute-start | bytes 49160 | tf_op jit(solution)/shard_map/ppermute | solution.py:235
  6.2 3.2 %collective-permute-start.2 = (f32[32,128]{1,0:T(8,128)S(1)}, f32[32,128]{1,0:T(8,128)S(1)}, u32[]{:S(2)}, u32[]{:S(2)}) collective-permute-start(f32[32,128]{1,0:T(8,128)S(1)} %shard_map.48), channel_id=1, source_target_pairs={{0,3},{1,2},{2,1},{3,0},{4,7},{5,6},{6,5},{7,4},{8,11},{9,10},{10,... | collective-permute-start | bytes 49160 | tf_op jit(solution)/shard_map/ppermute | solution.py:235
  6.9 2.4 %copy-start = (bf16[1,4,64,4096]{3,2,1,0:T(8,128)(2,1)S(1)}, bf16[1,4,64,4096]{3,2,1,0:T(8,128)(2,1)}, u32[]{:S(2)}) copy-start(bf16[1,4,64,4096]{3,2,1,0:T(8,128)(2,1)} %param.7) | copy-start | bytes 6291460
  9.7 7.9 %collective-permute-start.3 = (bf16[32,4096]{1,0:T(8,128)(2,1)S(1)}, bf16[32,4096]{1,0:T(8,128)(2,1)S(1)}, u32[]{:S(2)}, u32[]{:S(2)}) collective-permute-start(bf16[32,4096]{1,0:T(8,128)(2,1)S(1)} %get-tuple-element.83.refs_1_), channel_id=1, source_target_pairs={{0,4},{1,5},{2,6},{3,7}} | collective-permute-start | bytes 786440 | tf_op jit(solution)/shard_map/ppermute | solution.py:235
  10.4 16.0 %collective-permute-start.11 = (bf16[64,4096]{1,0:T(8,128)(2,1)S(1)}, bf16[64,4096]{1,0:T(8,128)(2,1)S(1)}, u32[]{:S(2)}, u32[]{:S(2)}) collective-permute-start(bf16[64,4096]{1,0:T(8,128)(2,1)S(1)} %bitcast.38), channel_id=1, source_target_pairs={{12,8},{13,9},{14,10},{15,11},{16,12},{17,13},{18,14},{19,15},{20,... | collective-permute-start | bytes 1572872 | tf_op jit(solution)/shard_map/ppermute | solution.py:235
  16.3 2.4 %collective-permute-start.5 = (f32[32,128]{1,0:T(8,128)S(1)}, f32[32,128]{1,0:T(8,128)S(1)}, u32[]{:S(2)}, u32[]{:S(2)}) collective-permute-start(f32[32,128]{1,0:T(8,128)S(1)} %shard_map.50.refs_0_), channel_id=1, source_target_pairs={{0,6},{1,7},{2,4},{3,5}} | collective-permute-start | bytes 49160 | tf_op jit(solution)/shard_map/ppermute | solution.py:235
  17.0 1.7 %collective-permute-start.6 = (f32[32,128]{1,0:T(8,128)S(1)}, f32[32,128]{1,0:T(8,128)S(1)}, u32[]{:S(2)}, u32[]{:S(2)}) collective-permute-start(f32[32,128]{1,0:T(8,128)S(1)} %shard_map.50.refs_0_), channel_id=1, source_target_pairs={{0,7},{1,6},{2,5},{3,4}} | collective-permute-start | bytes 49160 | tf_op jit(solution)/shard_map/ppermute | solution.py:235
  18.0 2.5 %collective-permute-start.7 = (f32[32,128]{1,0:T(8,128)S(1)}, f32[32,128]{1,0:T(8,128)S(1)}, u32[]{:S(2)}, u32[]{:S(2)}) collective-permute-start(f32[32,128]{1,0:T(8,128)S(1)} %shard_map.53), channel_id=1, source_target_pairs={{4,5},{5,4},{6,7},{7,6}} | collective-permute-start | bytes 49160 | tf_op jit(solution)/shard_map/ppermute | solution.py:235
  20.9 5.5 %collective-permute-start.8 = (bf16[32,4096]{1,0:T(8,128)(2,1)S(1)}, bf16[32,4096]{1,0:T(8,128)(2,1)S(1)}, u32[]{:S(2)}, u32[]{:S(2)}) collective-permute-start(bf16[32,4096]{1,0:T(8,128)(2,1)S(1)} %get-tuple-element.91.refs_1_), channel_id=1, source_target_pairs={{4,8},{5,9},{6,10},{7,11}} | collective-permute-start | bytes 786440 | tf_op jit(solution)/shard_map/ppermute | solution.py:235
  21.9 5.5 %collective-permute-start.10 = (f32[32,128]{1,0:T(8,128)S(1)}, f32[32,128]{1,0:T(8,128)S(1)}, u32[]{:S(2)}, u32[]{:S(2)}) collective-permute-start(f32[32,128]{1,0:T(8,128)S(1)} %shard_map.55), channel_id=1, source_target_pairs={{4,11},{5,10},{6,9},{7,8}} | collective-permute-start | bytes 49160 | tf_op jit(solution)/shard_map/ppermute | solution.py:235
  22.6 4.9 %collective-permute-start.9 = (f32[32,128]{1,0:T(8,128)S(1)}, f32[32,128]{1,0:T(8,128)S(1)}, u32[]{:S(2)}, u32[]{:S(2)}) collective-permute-start(f32[32,128]{1,0:T(8,128)S(1)} %shard_map.55), channel_id=1, source_target_pairs={{4,10},{5,11},{6,8},{7,9}} | collective-permute-start | bytes 49160 | tf_op jit(solution)/shard_map/ppermute | solution.py:235
  26.8 2.5 %collective-permute-start.12 = (f32[32,128]{1,0:T(8,128)S(1)}, f32[32,128]{1,0:T(8,128)S(1)}, u32[]{:S(2)}, u32[]{:S(2)}) collective-permute-start(f32[32,128]{1,0:T(8,128)S(1)} %shard_map.58), channel_id=1, source_target_pairs={{8,9},{9,8},{10,11},{11,10}} | collective-permute-start | bytes 49160 | tf_op jit(solution)/shard_map/ppermute | solution.py:235
  29.6 4.1 %collective-permute-start.13 = (bf16[32,2048]{1,0:T(8,128)(2,1)S(1)}, bf16[32,2048]{1,0:T(8,128)(2,1)S(1)}, u32[]{:S(2)}, u32[]{:S(2)}) collective-permute-start(bf16[32,2048]{1,0:T(8,128)(2,1)S(1)} %get-tuple-element.98.refs_2_), channel_id=1, source_target_pairs={{8,12},{9,13},{10,14},{11,15}} | collective-permute-start | bytes 393224 | tf_op jit(solution)/shard_map/ppermute | solution.py:235
  30.5 4.1 %collective-permute-start.14 = (bf16[32,2048]{1,0:T(8,128)(2,1)S(1)}, bf16[32,2048]{1,0:T(8,128)(2,1)S(1)}, u32[]{:S(2)}, u32[]{:S(2)}) collective-permute-start(bf16[32,2048]{1,0:T(8,128)(2,1)S(1)} %get-tuple-element.104.refs_3_), channel_id=1, source_target_pairs={{8,12},{9,13},{10,14},{11,15}} | collective-permute-start | bytes 393224 | tf_op jit(solution)/shard_map/ppermute | solution.py:235
  31.6 3.9 %collective-permute-start.15 = (f32[32,128]{1,0:T(8,128)S(1)}, f32[32,128]{1,0:T(8,128)S(1)}, u32[]{:S(2)}, u32[]{:S(2)}) collective-permute-start(f32[32,128]{1,0:T(8,128)S(1)} %shard_map.63), channel_id=1, source_target_pairs={{8,13},{9,12},{10,15},{11,14}} | collective-permute-start | bytes 49160 | tf_op jit(solution)/shard_map/ppermute | solution.py:235
  32.3 3.2 %collective-permute-start.16 = (f32[32,128]{1,0:T(8,128)S(1)}, f32[32,128]{1,0:T(8,128)S(1)}, u32[]{:S(2)}, u32[]{:S(2)}) collective-permute-start(f32[32,128]{1,0:T(8,128)S(1)} %shard_map.63), channel_id=1, source_target_pairs={{8,14},{9,15},{10,12},{11,13}} | collective-permute-start | bytes 49160 | tf_op jit(solution)/shard_map/ppermute | solution.py:235
  33.0 2.5 %collective-permute-start.17 = (f32[32,128]{1,0:T(8,128)S(1)}, f32[32,128]{1,0:T(8,128)S(1)}, u32[]{:S(2)}, u32[]{:S(2)}) collective-permute-start(f32[32,128]{1,0:T(8,128)S(1)} %shard_map.63), channel_id=1, source_target_pairs={{8,15},{9,14},{10,13},{11,12}} | collective-permute-start | bytes 49160 | tf_op jit(solution)/shard_map/ppermute | solution.py:235
  35.9 3.2 %collective-permute-start.18 = (bf16[32,4096]{1,0:T(8,128)(2,1)S(1)}, bf16[32,4096]{1,0:T(8,128)(2,1)S(1)}, u32[]{:S(2)}, u32[]{:S(2)}) collective-permute-start(bf16[32,4096]{1,0:T(8,128)(2,1)S(1)} %get-tuple-element.109.refs_2_), channel_id=1, source_target_pairs={{12,16},{13,17},{14,18},{15,19}} | collective-permute-start | bytes 786440 | tf_op jit(solution)/shard_map/ppermute | solution.py:235
  37.0 3.9 %collective-permute-start.19 = (f32[32,128]{1,0:T(8,128)S(1)}, f32[32,128]{1,0:T(8,128)S(1)}, u32[]{:S(2)}, u32[]{:S(2)}) collective-permute-start(f32[32,128]{1,0:T(8,128)S(1)} %shard_map.67), channel_id=1, source_target_pairs={{12,17},{13,16},{14,19},{15,18}} | collective-permute-start | bytes 49160 | tf_op jit(solution)/shard_map/ppermute | solution.py:235
  37.8 3.2 %collective-permute-start.20 = (f32[32,128]{1,0:T(8,128)S(1)}, f32[32,128]{1,0:T(8,128)S(1)}, u32[]{:S(2)}, u32[]{:S(2)}) collective-permute-start(f32[32,128]{1,0:T(8,128)S(1)} %shard_map.67), channel_id=1, source_target_pairs={{12,18},{13,19},{14,16},{15,17}} | collective-permute-start | bytes 49160 | tf_op jit(solution)/shard_map/ppermute | solution.py:235
  38.4 2.5 %collective-permute-start.21 = (f32[32,128]{1,0:T(8,128)S(1)}, f32[32,128]{1,0:T(8,128)S(1)}, u32[]{:S(2)}, u32[]{:S(2)}) collective-permute-start(f32[32,128]{1,0:T(8,128)S(1)} %shard_map.67), channel_id=1, source_target_pairs={{12,19},{13,18},{14,17},{15,16}} | collective-permute-start | bytes 49160 | tf_op jit(solution)/shard_map/ppermute | solution.py:235
  41.2 4.3 %collective-permute-start.22 = (bf16[32,2048]{1,0:T(8,128)(2,1)S(1)}, bf16[32,2048]{1,0:T(8,128)(2,1)S(1)}, u32[]{:S(2)}, u32[]{:S(2)}) collective-permute-start(bf16[32,2048]{1,0:T(8,128)(2,1)S(1)} %get-tuple-element.116.refs_2_), channel_id=1, source_target_pairs={{16,20},{17,21},{18,22},{19,23}} | collective-permute-start | bytes 393224 | tf_op jit(solution)/shard_map/ppermute | solution.py:235
  42.2 4.3 %collective-permute-start.23 = (bf16[32,2048]{1,0:T(8,128)(2,1)S(1)}, bf16[32,2048]{1,0:T(8,128)(2,1)S(1)}, u32[]{:S(2)}, u32[]{:S(2)}) collective-permute-start(bf16[32,2048]{1,0:T(8,128)(2,1)S(1)} %get-tuple-element.122.refs_3_), channel_id=1, source_target_pairs={{16,20},{17,21},{18,22},{19,23}} | collective-permute-start | bytes 393224 | tf_op jit(solution)/shard_map/ppermute | solution.py:235
  43.3 4.1 %collective-permute-start.24 = (f32[32,128]{1,0:T(8,128)S(1)}, f32[32,128]{1,0:T(8,128)S(1)}, u32[]{:S(2)}, u32[]{:S(2)}) collective-permute-start(f32[32,128]{1,0:T(8,128)S(1)} %shard_map.72), channel_id=1, source_target_pairs={{16,21},{17,20},{18,23},{19,22}} | collective-permute-start | bytes 49160 | tf_op jit(solution)/shard_map/ppermute | solution.py:235
  44.0 3.4 %collective-permute-start.25 = (f32[32,128]{1,0:T(8,128)S(1)}, f32[32,128]{1,0:T(8,128)S(1)}, u32[]{:S(2)}, u32[]{:S(2)}) collective-permute-start(f32[32,128]{1,0:T(8,128)S(1)} %shard_map.72), channel_id=1, source_target_pairs={{16,22},{17,23},{18,20},{19,21}} | collective-permute-start | bytes 49160 | tf_op jit(solution)/shard_map/ppermute | solution.py:235
  44.7 2.7 %collective-permute-start.26 = (f32[32,128]{1,0:T(8,128)S(1)}, f32[32,128]{1,0:T(8,128)S(1)}, u32[]{:S(2)}, u32[]{:S(2)}) collective-permute-start(f32[32,128]{1,0:T(8,128)S(1)} %shard_map.72), channel_id=1, source_target_pairs={{16,23},{17,22},{18,21},{19,20}} | collective-permute-start | bytes 49160 | tf_op jit(solution)/shard_map/ppermute | solution.py:235
  47.8 3.2 %collective-permute-start.27 = (bf16[32,4096]{1,0:T(8,128)(2,1)S(1)}, bf16[32,4096]{1,0:T(8,128)(2,1)S(1)}, u32[]{:S(2)}, u32[]{:S(2)}) collective-permute-start(bf16[32,4096]{1,0:T(8,128)(2,1)S(1)} %get-tuple-element.127.refs_2_), channel_id=1, source_target_pairs={{20,24},{21,25},{22,26},{23,27}} | collective-permute-start | bytes 786440 | tf_op jit(solution)/shard_map/ppermute | solution.py:235
  48.9 3.9 %collective-permute-start.28 = (f32[32,128]{1,0:T(8,128)S(1)}, f32[32,128]{1,0:T(8,128)S(1)}, u32[]{:S(2)}, u32[]{:S(2)}) collective-permute-start(f32[32,128]{1,0:T(8,128)S(1)} %shard_map.76), channel_id=1, source_target_pairs={{20,25},{21,24},{22,27},{23,26}} | collective-permute-start | bytes 49160 | tf_op jit(solution)/shard_map/ppermute | solution.py:235
  49.6 3.2 %collective-permute-start.29 = (f32[32,128]{1,0:T(8,128)S(1)}, f32[32,128]{1,0:T(8,128)S(1)}, u32[]{:S(2)}, u32[]{:S(2)}) collective-permute-start(f32[32,128]{1,0:T(8,128)S(1)} %shard_map.76), channel_id=1, source_target_pairs={{20,26},{21,27},{22,24},{23,25}} | collective-permute-start | bytes 49160 | tf_op jit(solution)/shard_map/ppermute | solution.py:235
  50.3 2.5 %collective-permute-start.30 = (f32[32,128]{1,0:T(8,128)S(1)}, f32[32,128]{1,0:T(8,128)S(1)}, u32[]{:S(2)}, u32[]{:S(2)}) collective-permute-start(f32[32,128]{1,0:T(8,128)S(1)} %shard_map.76), channel_id=1, source_target_pairs={{20,27},{21,26},{22,25},{23,24}} | collective-permute-start | bytes 49160 | tf_op jit(solution)/shard_map/ppermute | solution.py:235
  53.1 39.6 %collective-permute-start.31 = (bf16[32,2048]{1,0:T(8,128)(2,1)S(1)}, bf16[32,2048]{1,0:T(8,128)(2,1)S(1)}, u32[]{:S(2)}, u32[]{:S(2)}) collective-permute-start(bf16[32,2048]{1,0:T(8,128)(2,1)S(1)} %get-tuple-element.134.refs_2_), channel_id=1, source_target_pairs={{24,28},{25,29},{26,30},{27,31}} | collective-permute-start | bytes 393224 | tf_op jit(solution)/shard_map/ppermute | solution.py:235
  54.7 39.9 %collective-permute-start.32 = (bf16[32,2048]{1,0:T(8,128)(2,1)S(1)}, bf16[32,2048]{1,0:T(8,128)(2,1)S(1)}, u32[]{:S(2)}, u32[]{:S(2)}) collective-permute-start(bf16[32,2048]{1,0:T(8,128)(2,1)S(1)} %get-tuple-element.139.refs_3_), channel_id=1, source_target_pairs={{24,28},{25,29},{26,30},{27,31}} | collective-permute-start | bytes 393224 | tf_op jit(solution)/shard_map/ppermute | solution.py:235
  56.4 39.1 %collective-permute-start.33 = (f32[32,128]{1,0:T(8,128)S(1)}, f32[32,128]{1,0:T(8,128)S(1)}, u32[]{:S(2)}, u32[]{:S(2)}) collective-permute-start(f32[32,128]{1,0:T(8,128)S(1)} %shard_map.81), channel_id=1, source_target_pairs={{24,29},{25,28},{26,31},{27,30}} | collective-permute-start | bytes 49160 | tf_op jit(solution)/shard_map/ppermute | solution.py:235
  57.7 38.5 %collective-permute-start.34 = (f32[32,128]{1,0:T(8,128)S(1)}, f32[32,128]{1,0:T(8,128)S(1)}, u32[]{:S(2)}, u32[]{:S(2)}) collective-permute-start(f32[32,128]{1,0:T(8,128)S(1)} %shard_map.81), channel_id=1, source_target_pairs={{24,30},{25,31},{26,28},{27,29}} | collective-permute-start | bytes 49160 | tf_op jit(solution)/shard_map/ppermute | solution.py:235
  59.0 37.2 %collective-permute-start.35 = (f32[32,128]{1,0:T(8,128)S(1)}, f32[32,128]{1,0:T(8,128)S(1)}, u32[]{:S(2)}, u32[]{:S(2)}) collective-permute-start(f32[32,128]{1,0:T(8,128)S(1)} %shard_map.81), channel_id=1, source_target_pairs={{24,31},{25,30},{26,29},{27,28}} | collective-permute-start | bytes 49160 | tf_op jit(solution)/shard_map/ppermute | solution.py:235
